TPU v7x, 32 devices: a whole 2x2x4 slice. The times are simulated.
32 devices in a mesh: seq: 8 (over z, x), head: 4 (over y, core).
Axes of the slice: x: 2, y: 2, z: 4, core: 2. Of those that a mesh axis runs over, the one named last changes fastest.
Arguments:
- tokens: bfloat16 [1024, 4, 2048], P('seq', None, 'head'), may hold values from -6 to 6
- attn_gain: bfloat16 [2048], replicated, may hold values from 0.25 to 1.75
- query_weight: bfloat16 [2048, 2048], P(None, 'head'), may hold values from -0.125 to 0.125
- key_weight: bfloat16 [2048, 2048], P(None, 'head'), may hold values from -0.125 to 0.125
- value_weight: bfloat16 [2048, 2048], P(None, 'head'), may hold values from -0.125 to 0.125
- head_gain: bfloat16 [2048], P('head'), may hold values from 0.25 to 1.75
- out_weight: bfloat16 [2048, 2048], P('head'), may hold values from -0.125 to 0.125
- moe_gain: bfloat16 [2048], replicated, may hold values from 0.25 to 1.75
- route_ids: int32 [1024, 4, 8], P(('seq', 'head')), may hold values from 0 to 63, all different within a row; in each aligned block of 128 rows (0 to 127, 128 to 255, ..., all dimensions but the last counted through in order) at most 24 rows name the same one
- route_weight: float32 [1024, 4, 8], P(('seq', 'head')), may hold values from 0.05 to 0.3
- expert_gate: bfloat16 [128, 2048, 512], P(('seq', 'head')), may hold values from -0.125 to 0.125
- expert_up: bfloat16 [128, 2048, 512], P(('seq', 'head')), may hold values from -0.125 to 0.125
- expert_down: bfloat16 [128, 512, 2048], P(('seq', 'head')), may hold values from -0.1875 to 0.1875
Outputs:
- layer_output: bfloat16 [1024, 4, 2048], P(('seq', 'head'))
Inputs may be any that keep to these rules, and one draw needn't show every extreme that they name: `route_ids`: the rows [position, sequence] taken position-major form aligned blocks of 128 rows, the rows of one device; within every block no expert is named by more than 24 routes, and in every draw some block has an expert named by exactly 24 routes. The 8 experts of a row differ.
All inputs are finite; a program needn't handle non-finite values.
Results may differ from a plain program's by a relative error of at most 0.017.
Values may be sent and summed in bfloat16 or wider, within the bound.
A program may use at most 128 MiB of HBM per device.

v0:
```python
import jax
import jax.numpy as jnp
from jax import lax
from jax.sharding import PartitionSpec as P

HEAD_DIM = 128
EXPERTS = 64
TOP = 8


norm_eps = 1e-05
head_eps = 1e-06


def passed_along(x, axis, by):
    count = lax.axis_size(axis)
    pairs = [(i, i + by) for i in range(count) if 0 <= i + by < count]
    return lax.ppermute(x, axis, pairs)


def swapped(block, axis, apart):
    count = lax.axis_size(axis)
    route = []
    for low in range(count):
        high = low | 1 << apart
        if high != low and high < count:
            route += [(low, high), (high, low)]
    return lax.ppermute(block, axis, route)


def root_scale(values, gain_values, epsilon):
    return (
        values
        * lax.rsqrt(jnp.mean(values * values, axis=-1, keepdims=True) + epsilon)
        * gain_values.astype(jnp.float32)
    )


def body(
    tokens,
    attn_gain,
    query_weight,
    key_weight,
    value_weight,
    head_gain,
    out_weight,
    moe_gain,
    route_ids,
    route_weight,
    expert_gate,
    expert_up,
    expert_down,
):
    head_count = lax.axis_size("head")
    seq_count = lax.axis_size("seq")
    gathered = lax.all_gather(tokens, "head", axis=2, tiled=True)
    block_len, batch_size, model_width = gathered.shape
    stream = gathered.astype(jnp.float32)
    normed = root_scale(stream, attn_gain, norm_eps).astype(jnp.bfloat16)
    heads_local = query_weight.shape[1] // HEAD_DIM
    head_shape = (block_len, batch_size, heads_local, HEAD_DIM)

    def project(weight):
        return jnp.dot(normed, weight, preferred_element_type=jnp.float32)

    query_rows = jax.nn.silu(project(query_weight)).astype(jnp.bfloat16).reshape(head_shape)
    key_rows = jax.nn.silu(project(key_weight)).astype(jnp.bfloat16).reshape(head_shape)
    value_rows = project(value_weight).astype(jnp.bfloat16).reshape(head_shape)
    position = lax.broadcasted_iota(jnp.int32, (block_len, block_len), 0)
    key_position = lax.broadcasted_iota(jnp.int32, (block_len, block_len), 1)
    scores = jnp.einsum("pbhd,sbhd->bhps", query_rows, key_rows, preferred_element_type=jnp.float32)
    scores = jnp.where(position >= key_position, scores, 0.0).astype(jnp.bfloat16)
    local_mix = jnp.einsum(
        "bhps,sbhd->pbhd", scores, value_rows, preferred_element_type=jnp.float32
    )
    local_state = jnp.einsum(
        "sbhd,sbhe->bhde", key_rows, value_rows, preferred_element_type=jnp.float32
    )

    def pass_state(step_index, carried_pair):
        incoming = passed_along(carried_pair[1].astype(jnp.bfloat16), "seq", 1).astype(jnp.float32)
        return (incoming, incoming + local_state)

    carried, unused_total = lax.fori_loop(
        0, seq_count - 1, pass_state, (jnp.zeros_like(local_state), local_state)
    )
    carried_mix = jnp.einsum(
        "pbhd,bhde->pbhe", query_rows.astype(jnp.float32), carried, precision=lax.Precision.HIGHEST
    )
    mixed_heads = local_mix + carried_mix
    attended = root_scale(mixed_heads, head_gain.reshape(heads_local, HEAD_DIM), head_eps).astype(
        jnp.bfloat16
    )
    attended = attended.reshape(block_len, batch_size, heads_local * HEAD_DIM)
    own_rows = block_len // head_count
    row_term = jnp.dot(attended, out_weight, preferred_element_type=jnp.float32).astype(
        jnp.bfloat16
    )
    projected = lax.psum_scatter(
        lax.optimization_barrier(row_term).astype(jnp.float32).astype(jnp.bfloat16),
        "head",
        scatter_dimension=0,
        tiled=True,
    ).astype(jnp.float32)
    own_stream = lax.dynamic_slice_in_dim(stream, lax.axis_index("head") * own_rows, own_rows, 0)
    total_rows = own_rows * batch_size
    residual_stream = (own_stream + projected).reshape(total_rows, model_width)
    moe_input = root_scale(residual_stream, moe_gain, norm_eps).astype(jnp.bfloat16)
    capacity = max(2, 3 * total_rows * TOP // (2 * EXPERTS))
    expert_ids = route_ids.reshape(total_rows * TOP)
    one_hot = (expert_ids[:, None] == jnp.arange(EXPERTS, dtype=jnp.int32)[None, :]).astype(
        jnp.int32
    )
    running = jnp.cumsum(one_hot, axis=0)
    expert_slot = jnp.sum(running * one_hot, axis=1) - 1
    flat_slot = expert_ids * capacity + expert_slot
    repeated = jnp.repeat(moe_input, TOP, axis=0)
    dispatch = (
        jnp.zeros((EXPERTS * capacity, model_width), jnp.bfloat16).at[flat_slot].set(repeated)
    )
    dispatch = dispatch.reshape(EXPERTS, capacity, model_width)
    device_count = seq_count * head_count
    halves_local = expert_gate.shape[0]
    device_rank = lax.axis_index("seq") * head_count + lax.axis_index("head")
    parity = (device_rank * halves_local + jnp.arange(halves_local, dtype=jnp.int32)) % 2
    lower_half = (parity == 0)[:, None, None, None]
    sending = jnp.broadcast_to(dispatch[:, None], (EXPERTS, 2, capacity, model_width)).reshape(
        2 * EXPERTS, capacity, model_width
    )
    received = lax.all_to_all(sending, ("seq", "head"), split_axis=0, concat_axis=1, tiled=True)
    gate_rows = jnp.einsum(
        "lmd,ldf->lmf", received, expert_gate, preferred_element_type=jnp.float32
    )
    up_rows = jnp.einsum("lmd,ldf->lmf", received, expert_up, preferred_element_type=jnp.float32)
    activated = (jax.nn.silu(gate_rows) * up_rows).astype(jnp.bfloat16)
    half_output = jnp.einsum(
        "lmf,lfd->lmd", activated, expert_down, preferred_element_type=jnp.float32
    ).astype(jnp.bfloat16)
    if halves_local >= 2:
        other_output = half_output.reshape(
            halves_local // 2, 2, device_count * capacity, model_width
        )[:, ::-1]
        other_output = other_output.reshape(half_output.shape)
    else:
        other_output = swapped(half_output, "head", 0)
    summed = (half_output.astype(jnp.float32) + other_output.astype(jnp.float32)).astype(
        jnp.bfloat16
    )
    summed = summed.reshape(halves_local, device_count, capacity, model_width)
    kept = jnp.where(lower_half, summed[:, :, : capacity // 2], summed[:, :, capacity // 2 :])
    kept = kept.reshape(halves_local, device_count * capacity // 2, model_width)
    returned = lax.all_to_all(kept, ("seq", "head"), split_axis=1, concat_axis=0, tiled=True)
    paired = returned.reshape(EXPERTS, 2, capacity // 2, model_width)
    expert_sum = jnp.concatenate([paired[:, 0], paired[:, 1]], axis=1)
    expert_sum = expert_sum.reshape(EXPERTS * capacity, model_width)
    picked = (
        expert_sum[flat_slot].astype(jnp.float32) * route_weight.reshape(total_rows * TOP)[:, None]
    )
    moe_output = jnp.sum(picked.reshape(total_rows, TOP, model_width), axis=1)
    return (
        (residual_stream + moe_output)
        .astype(jnp.bfloat16)
        .reshape(own_rows, batch_size, model_width)
    )


def solution(mesh):
    in_specs = (
        P("seq", None, "head"),
        P(),
        P(None, "head"),
        P(None, "head"),
        P(None, "head"),
        P("head"),
        P("head", None),
        P(),
        P(("seq", "head"), None, None),
        P(("seq", "head"), None, None),
        P(("seq", "head"), None, None),
        P(("seq", "head"), None, None),
        P(("seq", "head"), None, None),
    )
    out_specs = P(("seq", "head"), None, None)
    return jax.shard_map(body, mesh=mesh, in_specs=in_specs, out_specs=out_specs, check_vma=False)
```

profile of v0, /device:TPU:0, one launch (start us, length us, event | category | flops | bytes accessed | tf_op | source)
XLA Modules:
  0.0 836.0 jit_solution(2850672741767305803)
XLA Ops:
  6.5 2.1 copy.86
  8.7 0.7 convert_element_type.90
  9.4 0.7 bitcast_convert_fusion
  10.1 24.2 %all-gather.2.cloned.1.call-done = bf16[128,4,2048]{2,0,1:T(8,128)(2,1)} async-done(((bf16[128,4,512]{2,0,1:T(8,128)(2,1)}), bf16[128,4,2048]{2,0,1:T(8,128)(2,1)}) %all-gather.2.cloned.1.call-update) | async-done | bytes 2097168 | tf_op jit(solution)/shard_map/all_gather | solution.py:56
  34.2 2.1 multiply_reduce_fusion
  36.3 3.7 multiply_convert_fusion.8
  40.0 1.0 copy.116
  41.0 3.7 fusion.22
  44.7 1.1 fusion.56
  45.8 2.3 fusion.28
  48.1 2.9 fusion.21
  51.0 116.4 %while.13 = (s32[]{:T(128)}, f32[4,4,128,128]{3,2,1,0:T(8,128)}, bf16[4,4,128,128]{3,2,1,0:T(8,128)(2,1)}, f32[4,4,128,128]{3,2,1,0:T(8,128)S(1)}) while((s32[]{:T(128)}, f32[4,4,128,128]{3,2,1,0:T(8,128)}, bf16[4,4,128,128]{3,2,1,0:T(8,128)(2,1)}, f32[4,4,128,128]{3,2,1,0:T(8,128)S(1)}) %tuple.31), condition=%wide.region_2.3_spmd.clone, body=%wide.region_1.2_spmd.sunk.clone | while | flops 1048578 | bytes 5242973 | solution.py:84
  51.2 4.2 collective-permute-start
  55.4 11.1 %collective-permute-done = bf16[4,4,128,128]{3,2,1,0:T(8,128)(2,1)} collective-permute-done((bf16[4,4,128,128]{3,2,1,0:T(8,128)(2,1)}, bf16[4,4,128,128]{3,2,1,0:T(8,128)(2,1)}, u32[]{:S(2)}, u32[]{:S(2)}) %collective-permute-start) | collective-permute-done | bytes 524320 | tf_op jit(solution)/shard_map/while/body/eval_jaxpr/ppermute | solution.py:18
  66.5 2.6 fusion.69
  69.1 5.2 collective-permute-start
  74.2 10.3 %collective-permute-done = bf16[4,4,128,128]{3,2,1,0:T(8,128)(2,1)} collective-permute-done((bf16[4,4,128,128]{3,2,1,0:T(8,128)(2,1)}, bf16[4,4,128,128]{3,2,1,0:T(8,128)(2,1)}, u32[]{:S(2)}, u32[]{:S(2)}) %collective-permute-start) | collective-permute-done | bytes 524320 | tf_op jit(solution)/shard_map/while/body/eval_jaxpr/ppermute | solution.py:18
  84.5 2.6 fusion.69
  87.1 5.2 collective-permute-start
  92.3 9.4 %collective-permute-done = bf16[4,4,128,128]{3,2,1,0:T(8,128)(2,1)} collective-permute-done((bf16[4,4,128,128]{3,2,1,0:T(8,128)(2,1)}, bf16[4,4,128,128]{3,2,1,0:T(8,128)(2,1)}, u32[]{:S(2)}, u32[]{:S(2)}) %collective-permute-start) | collective-permute-done | bytes 524320 | tf_op jit(solution)/shard_map/while/body/eval_jaxpr/ppermute | solution.py:18
  101.6 2.6 fusion.69
  104.2 6.0 collective-permute-start
  110.1 8.4 %collective-permute-done = bf16[4,4,128,128]{3,2,1,0:T(8,128)(2,1)} collective-permute-done((bf16[4,4,128,128]{3,2,1,0:T(8,128)(2,1)}, bf16[4,4,128,128]{3,2,1,0:T(8,128)(2,1)}, u32[]{:S(2)}, u32[]{:S(2)}) %collective-permute-start) | collective-permute-done | bytes 524320 | tf_op jit(solution)/shard_map/while/body/eval_jaxpr/ppermute | solution.py:18
  118.6 2.6 fusion.69
  121.1 6.1 collective-permute-start
  127.2 7.5 collective-permute-done
  134.7 2.6 fusion.69
  137.3 6.1 collective-permute-start
  143.4 6.6 collective-permute-done
  150.0 2.6 fusion.69
  152.5 6.1 collective-permute-start
  158.6 6.2 collective-permute-done
  164.8 2.6 fusion.69
  167.4 2.8 multiply_reduce_fusion.2
  170.4 2.6 convolution_convert_fusion.1
  173.4 18.0 %reduce-window.6 = s32[64,8,128]{2,1,0:T(8,128)S(1)} reduce-window(s32[64,8,128]{2,1,0:T(8,128)S(1)} %fusion.48, s32[]{:T(128)} %constant.28.clone.1), window={size=1x1x128 pad=0_0x0_0x127_0}, to_apply=%region_5.6 | reduce-window | flops 8323072 | bytes 524292 | tf_op jit(solution)/shard_map/reduce-window
  192.3 4.4 convert_element_type.89
  196.7 11.1 %reduce-scatter.2.cloned.1.call-done = bf16[32,4,2048]{2,0,1:T(8,128)(2,1)} async-done(((bf16[128,4,2048]{2,0,1:T(8,128)(2,1)}), bf16[32,4,2048]{2,0,1:T(8,128)(2,1)}) %reduce-scatter.2.cloned.1.call-update) | async-done | bytes 524304 | tf_op jit(solution)/shard_map/reduce_scatter | solution.py:99
  207.8 1.6 multiply_reduce_fusion.1
  210.8 10.1 %scatter_custom_fusion = bf16[1536,2048]{1,0:T(8,128)(2,1)} fusion(s32[1024]{0:T(1024)S(1)} %bitcast.116, bf16[]{:T(256)} %constant.68.clone.1, bf16[128,2048]{1,0:T(8,128)(2,1)S(1)} %multiply_convert_fusion.6), kind=kCustom, calls=%fused_computation.10 | custom fusion | bytes 6815746 | tf_op jit(solution)/shard_map/scatter | solution.py:119
  221.0 8.5 %broadcast_in_dim.46 = bf16[64,2,24,2048]{3,2,1,0:T(8,128)(2,1)} broadcast(bf16[64,24,2048]{2,1,0:T(8,128)(2,1)} %bitcast.107), dimensions={0,2,3} | broadcast | bytes 18874368 | tf_op jit(solution)/shard_map/broadcast_in_dim | solution.py:127
  229.5 5.2 all-to-all-start
  234.7 275.5 %all-to-all-done = bf16[128,24,2048]{2,1,0:T(8,128)(2,1)} async-done(((bf16[128,24,2048]{2,1,0:T(8,128)(2,1)}), bf16[128,24,2048]{2,1,0:T(8,128)(2,1)}, u32[]{:S(2)}, u32[]{:S(2)}) %all-to-all-start) | async-done | bytes 12582944 | tf_op jit(solution)/shard_map/all_to_all | solution.py:130
  510.2 6.2 copy.102
  516.4 4.5 copy-done.2
  520.9 10.8 %fusion.57 = f32[4,768,512]{2,1,0:T(8,128)} fusion(bf16[4,768,2048]{2,1,0:T(8,128)(2,1)S(1)} %bitcast.108, bf16[4,2048,512]{2,1,0:T(8,128)(2,1)} %param.25), kind=kOutput, calls=%fused_computation.83 | convolution fusion | flops 6442450944 | bytes 27262976 | tf_op jit(solution)/shard_map/lmd,ldf->lmf/dot_general | solution.py:131
  531.6 21.1 %convolution_convert_fusion = bf16[4,768,2048]{2,1,0:T(8,128)(2,1)} fusion(bf16[4,512,2048]{2,1,0:T(8,128)(2,1)} %param.27, f32[4,768,512]{2,1,0:T(8,128)} %fusion.57, bf16[4,768,2048]{2,1,0:T(8,128)(2,1)} %bitcast.109, bf16[4,2048,512]{2,1,0:T(8,128)(2,1)} %param.26), kind=kOutput, calls=%fused_computation.6 | convolution fusion | flops 12900630528 | bytes 48234496 | tf_op jit(solution)/shard_map/lmf,lfd->lmd/dot_general | solution.py:136
  552.7 10.7 %rev.3 = bf16[2,2,768,2048]{3,2,1,0:T(8,128)(2,1)} reverse(bf16[2,2,768,2048]{3,2,1,0:T(8,128)(2,1)} %bitcast.105), dimensions={1} | reverse | bytes 25165824 | tf_op jit(solution)/shard_map/rev | solution.py:140
  563.5 10.8 %fusion = bf16[4,768,2048]{2,1,0:T(8,128)(2,1)S(1)} fusion(bf16[4,768,2048]{2,1,0:T(8,128)(2,1)} %convolution_convert_fusion, bf16[2,2,768,2048]{3,2,1,0:T(8,128)(2,1)} %rev.3), kind=kLoop, calls=%fused_computation.3 | loop fusion | flops 25165824 | bytes 37748736 | tf_op jit(solution)/shard_map/convert_element_type | solution.py:146
  574.3 5.0 fusion.54
  579.3 17.7 %copy_select_fusion = bf16[4,32,12,2048]{3,0,2,1:T(4,128)(2,1)} fusion(bf16[4,32,12,2048]{3,2,1,0:T(8,128)(2,1)S(1)} %get-tuple-element.40, bf16[4,32,12,2048]{3,2,1,0:T(8,128)(2,1)S(1)} %get-tuple-element.39, pred[4]{0:T(512)(128)(4,1)S(1)} %fusion.49), kind=kLoop, calls=%fused_computation.8 | loop fusion | flops 3145728 | bytes 18874372 | tf_op jit(solution)/shard_map/jit(_where)/select_n | solution.py:150
  597.0 11.9 %all-to-all-start.1 = ((bf16[4,384,2048]{2,0,1:T(4,128)(2,1)}), bf16[4,384,2048]{2,0,1:T(4,128)(2,1)}, u32[]{:S(2)}, u32[]{:S(2)}) async-start(bf16[4,384,2048]{2,0,1:T(4,128)(2,1)} %bitcast.106), calls=%async_computation.2 | async-start | bytes 12582912 | tf_op jit(solution)/shard_map/all_to_all | solution.py:152
  609.0 139.9 %all-to-all-done.1 = bf16[4,384,2048]{2,0,1:T(4,128)(2,1)} async-done(((bf16[4,384,2048]{2,0,1:T(4,128)(2,1)}), bf16[4,384,2048]{2,0,1:T(4,128)(2,1)}, u32[]{:S(2)}, u32[]{:S(2)}) %all-to-all-start.1) | async-done | bytes 6291488 | tf_op jit(solution)/shard_map/all_to_all | solution.py:152
  749.0 10.0 %copy.105 = bf16[32,4,12,2048]{3,1,0,2:T(4,128)(2,1)} copy(bf16[32,4,12,2048]{3,1,2,0:T(4,128)(2,1)} %bitcast.22) | data formatting | bytes 12582912 | tf_op jit(solution)/shard_map/all_to_all | solution.py:152
  758.9 13.6 %reshape.174 = bf16[64,2,12,2048]{3,1,0,2:T(2,128)(2,1)} reshape(bf16[32,4,12,2048]{3,1,0,2:T(4,128)(2,1)} %copy.105) | data formatting | bytes 12582912 | tf_op jit(solution)/shard_map/reshape | solution.py:153
  772.5 13.7 %fusion.55 = (bf16[64,1,12,2048]{3,1,0,2:T(2,128)(2,1)S(1)}, bf16[64,1,12,2048]{3,1,0,2:T(2,128)(2,1)}) fusion(bf16[64,2,12,2048]{3,1,0,2:T(2,128)(2,1)} %reshape.174), kind=kLoop, calls=%fused_computation.81 | loop fusion | bytes 12582912 | tf_op jit(solution)/shard_map/slice | solution.py:154
  786.2 8.5 %copy_bitcast_fusion = (bf16[64,12,2048]{2,0,1:T(8,128)(2,1)S(1)}, bf16[64,12,2048]{2,0,1:T(8,128)(2,1)}) fusion(bf16[64,1,12,2048]{3,1,0,2:T(2,128)(2,1)} %get-tuple-element.42, bf16[64,1,12,2048]{3,1,0,2:T(2,128)(2,1)S(1)} %get-tuple-element.41), kind=kLoop, calls=%fused_computation.15 | loop fusion | bytes 12582912
  794.7 2.4 pad_maximum_fusion
  797.1 6.1 copy.106
  803.2 12.7 %gather_fusion = bf16[1024,2048]{1,0:T(8,128)(2,1)} fusion(bf16[1536,2048]{1,0:T(8,128)(2,1)} %bitcast.102, s32[1024]{0:T(1024)S(1)} %broadcast_clamp_fusion), kind=kCustom, calls=%fused_computation | custom fusion | bytes 8392704 | tf_op jit(solution)/shard_map/gather | solution.py:157
  815.9 7.4 fusion.1
  823.4 2.5 reduce_sum.52
  825.9 1.8 fusion.25
  827.8 1.2 copy.109
  (54 shorter events, 3.0 us)
Async XLA Ops:
  6.5 163.8 %copy-start = (bf16[512,2048]{1,0:T(8,128)(2,1)S(1)}, bf16[512,2048]{1,0:T(8,128)(2,1)}, u32[]{:S(2)}) copy-start(bf16[512,2048]{1,0:T(8,128)(2,1)} %param.21) | copy-start | bytes 6291460
  6.5 27.7 %all-gather.2.cloned.1.call-start = ((), (), s32[]{:S(2)}) async-start(), calls=%async_computation.3 | async-start | bytes 2621440 | tf_op jit(solution)/shard_map/all_gather | solution.py:56
  8.6 199.1 %reduce-scatter.2.cloned.1.call-start = ((), (), s32[]{:S(2)}) async-start(), calls=%async_computation.4 | async-start | bytes 2621440 | tf_op jit(solution)/shard_map/reduce_scatter | solution.py:99
  41.0 3.7 copy-start.4
  41.0 4.8 copy-start.3
  41.0 4.8 copy-start.9
  44.7 1.1 copy-start.5
  51.2 15.3 %collective-permute-start = (bf16[4,4,128,128]{3,2,1,0:T(8,128)(2,1)}, bf16[4,4,128,128]{3,2,1,0:T(8,128)(2,1)}, u32[]{:S(2)}, u32[]{:S(2)}) collective-permute-start(bf16[4,4,128,128]{3,2,1,0:T(8,128)(2,1)} %get-tuple-element.93), channel_id=1, source_target_pairs={{0,4},{4,8},{8,12},{12,16},{16,20},{20,24},{24,28},{1,5},{5,9},{9,... | collective-permute-start | bytes 1572872 | tf_op jit(solution)/shard_map/while/body/eval_jaxpr/ppermute | solution.py:18
  69.1 15.4 %collective-permute-start = (bf16[4,4,128,128]{3,2,1,0:T(8,128)(2,1)}, bf16[4,4,128,128]{3,2,1,0:T(8,128)(2,1)}, u32[]{:S(2)}, u32[]{:S(2)}) collective-permute-start(bf16[4,4,128,128]{3,2,1,0:T(8,128)(2,1)} %get-tuple-element.93), channel_id=1, source_target_pairs={{0,4},{4,8},{8,12},{12,16},{16,20},{20,24},{24,28},{1,5},{5,9},{9,... | collective-permute-start | bytes 1572872 | tf_op jit(solution)/shard_map/while/body/eval_jaxpr/ppermute | solution.py:18
  87.1 14.5 %collective-permute-start = (bf16[4,4,128,128]{3,2,1,0:T(8,128)(2,1)}, bf16[4,4,128,128]{3,2,1,0:T(8,128)(2,1)}, u32[]{:S(2)}, u32[]{:S(2)}) collective-permute-start(bf16[4,4,128,128]{3,2,1,0:T(8,128)(2,1)} %get-tuple-element.93), channel_id=1, source_target_pairs={{0,4},{4,8},{8,12},{12,16},{16,20},{20,24},{24,28},{1,5},{5,9},{9,... | collective-permute-start | bytes 1572872 | tf_op jit(solution)/shard_map/while/body/eval_jaxpr/ppermute | solution.py:18
  104.2 14.4 %collective-permute-start = (bf16[4,4,128,128]{3,2,1,0:T(8,128)(2,1)}, bf16[4,4,128,128]{3,2,1,0:T(8,128)(2,1)}, u32[]{:S(2)}, u32[]{:S(2)}) collective-permute-start(bf16[4,4,128,128]{3,2,1,0:T(8,128)(2,1)} %get-tuple-element.93), channel_id=1, source_target_pairs={{0,4},{4,8},{8,12},{12,16},{16,20},{20,24},{24,28},{1,5},{5,9},{9,... | collective-permute-start | bytes 1572872 | tf_op jit(solution)/shard_map/while/body/eval_jaxpr/ppermute | solution.py:18
  121.1 13.6 %collective-permute-start = (bf16[4,4,128,128]{3,2,1,0:T(8,128)(2,1)}, bf16[4,4,128,128]{3,2,1,0:T(8,128)(2,1)}, u32[]{:S(2)}, u32[]{:S(2)}) collective-permute-start(bf16[4,4,128,128]{3,2,1,0:T(8,128)(2,1)} %get-tuple-element.93), channel_id=1, source_target_pairs={{0,4},{4,8},{8,12},{12,16},{16,20},{20,24},{24,28},{1,5},{5,9},{9,... | collective-permute-start | bytes 1572872 | tf_op jit(solution)/shard_map/while/body/eval_jaxpr/ppermute | solution.py:18
  137.3 12.7 %collective-permute-start = (bf16[4,4,128,128]{3,2,1,0:T(8,128)(2,1)}, bf16[4,4,128,128]{3,2,1,0:T(8,128)(2,1)}, u32[]{:S(2)}, u32[]{:S(2)}) collective-permute-start(bf16[4,4,128,128]{3,2,1,0:T(8,128)(2,1)} %get-tuple-element.93), channel_id=1, source_target_pairs={{0,4},{4,8},{8,12},{12,16},{16,20},{20,24},{24,28},{1,5},{5,9},{9,... | collective-permute-start | bytes 1572872 | tf_op jit(solution)/shard_map/while/body/eval_jaxpr/ppermute | solution.py:18
  152.5 12.3 %collective-permute-start = (bf16[4,4,128,128]{3,2,1,0:T(8,128)(2,1)}, bf16[4,4,128,128]{3,2,1,0:T(8,128)(2,1)}, u32[]{:S(2)}, u32[]{:S(2)}) collective-permute-start(bf16[4,4,128,128]{3,2,1,0:T(8,128)(2,1)} %get-tuple-element.93), channel_id=1, source_target_pairs={{0,4},{4,8},{8,12},{12,16},{16,20},{20,24},{24,28},{1,5},{5,9},{9,... | collective-permute-start | bytes 1572872 | tf_op jit(solution)/shard_map/while/body/eval_jaxpr/ppermute | solution.py:18
  167.4 5.7 copy-start.6
  167.4 6.0 copy-start.8
  229.5 280.7 %all-to-all-start = ((bf16[128,24,2048]{2,1,0:T(8,128)(2,1)}), bf16[128,24,2048]{2,1,0:T(8,128)(2,1)}, u32[]{:S(2)}, u32[]{:S(2)}) async-start(bf16[128,24,2048]{2,1,0:T(8,128)(2,1)} %bitcast.104), calls=%async_computation.1 | async-start | bytes 25165824 | tf_op jit(solution)/shard_map/all_to_all | solution.py:130
  516.4 4.5 copy-start.2
  597.0 11.9 %copy-start.7 = (f32[32,4,8]{0,2,1:T(8,128)S(1)}, f32[32,4,8]{0,2,1:T(8,128)}, u32[]{:S(2)}) copy-start(f32[32,4,8]{0,2,1:T(8,128)} %param.24) | copy-start | bytes 12292
  597.0 151.9 %all-to-all-start.1 = ((bf16[4,384,2048]{2,0,1:T(4,128)(2,1)}), bf16[4,384,2048]{2,0,1:T(4,128)(2,1)}, u32[]{:S(2)}, u32[]{:S(2)}) async-start(bf16[4,384,2048]{2,0,1:T(4,128)(2,1)} %bitcast.106), calls=%async_computation.2 | async-start | bytes 12582912 | tf_op jit(solution)/shard_map/all_to_all | solution.py:152
  803.2 25.8 %copy-start.1 = (bf16[512,2048]{1,0:T(8,128)(2,1)S(1)}, bf16[512,2048]{1,0:T(8,128)(2,1)}, u32[]{:S(2)}) copy-start(bf16[512,2048]{1,0:T(8,128)(2,1)} %param.21) | copy-start | bytes 6291460
Sparse Core Ops, SparseCore 0:
  8.9 25.2 all-gather.1
  173.2 34.5 reduce-scatter.1
where the time goes:
time: 842 us; the launch traced here: 836 us
  waiting for transfers between devices  510 us (61%)
  local copies, waits for them, and re-layouts  119 us (14%)
  other arithmetic  86.4 us (10%)
  starting transfers between devices  55.8 us (7%)
  matrix products  50.9 us (6%)
  between operations  14 us (2%)
    all_to_all x1, waiting for transfers between devices, body(): lax.all_to_all(sending, ('seq', 'head'), split_axis=0, concat_axis=1, til...  275 us
    all_to_all x1, waiting for transfers between devices, body(): lax.all_to_all(kept, ('seq', 'head'), split_axis=1, concat_axis=0, tiled=...  140 us
    ppermute x7, waiting for transfers between devices, passed_along(): return lax.ppermute(x, axis, pairs)  59.5 us
    ppermute x7, starting transfers between devices, passed_along(): return lax.ppermute(x, axis, pairs)  38.7 us
    all_gather x1, waiting for transfers between devices, body(): gathered = lax.all_gather(tokens, 'head', axis=2, tiled=True)  24.2 us
    dot_general x1, matrix products, body(): jnp.einsum('lmf,lfd->lmd', activated, expert_down, preferred_element_type...  21.1 us
    another operation x3, other arithmetic  18.2 us
    add x7, other arithmetic, pass_state(): return (incoming, incoming + local_state)  18 us
  transfers between devices with their start and end apart: 11, of which 11 were waited for; matrix products, arithmetic and copies ran while one was open for 3% of the time, Pallas kernels for 0%

commit v1 on v0

v1 whole, which is shorter than its diff:
```python
import jax
import jax.numpy as jnp
from jax import lax
from jax.sharding import PartitionSpec as P

HEAD_DIM = 128
EXPERTS = 64
TOP = 8


norm_eps = 1e-05
head_eps = 1e-06


def root_scale(values, gain_values, epsilon):
    return (
        values
        * lax.rsqrt(jnp.mean(values * values, axis=-1, keepdims=True) + epsilon)
        * gain_values.astype(jnp.float32)
    )


def body(
    tokens,
    attn_gain,
    query_weight,
    key_weight,
    value_weight,
    head_gain,
    out_weight,
    moe_gain,
    route_ids,
    route_weight,
    expert_gate,
    expert_up,
    expert_down,
):
    head_count = lax.axis_size("head")
    seq_count = lax.axis_size("seq")
    gathered = lax.all_gather(tokens, "head", axis=2, tiled=True)
    block_len, batch_size, model_width = gathered.shape
    stream = gathered.astype(jnp.float32)
    normed = root_scale(stream, attn_gain, norm_eps).astype(jnp.bfloat16)
    heads_local = query_weight.shape[1] // HEAD_DIM
    head_shape = (block_len, batch_size, heads_local, HEAD_DIM)

    def project(weight):
        return jnp.dot(normed, weight, preferred_element_type=jnp.float32)

    query_rows = jax.nn.silu(project(query_weight)).astype(jnp.bfloat16).reshape(head_shape)
    key_rows = jax.nn.silu(project(key_weight)).astype(jnp.bfloat16).reshape(head_shape)
    value_rows = project(value_weight).astype(jnp.bfloat16).reshape(head_shape)
    position = lax.broadcasted_iota(jnp.int32, (block_len, block_len), 0)
    key_position = lax.broadcasted_iota(jnp.int32, (block_len, block_len), 1)
    scores = jnp.einsum("pbhd,sbhd->bhps", query_rows, key_rows, preferred_element_type=jnp.float32)
    scores = jnp.where(position >= key_position, scores, 0.0).astype(jnp.bfloat16)
    local_mix = jnp.einsum(
        "bhps,sbhd->pbhd", scores, value_rows, preferred_element_type=jnp.float32
    )
    local_state = jnp.einsum(
        "sbhd,sbhe->bhde", key_rows, value_rows, preferred_element_type=jnp.float32
    )

    all_states = lax.all_gather(local_state.astype(jnp.bfloat16), "seq", axis=0, tiled=False)
    earlier = jnp.arange(seq_count, dtype=jnp.int32) < lax.axis_index("seq")
    carried = jnp.sum(
        jnp.where(earlier[:, None, None, None, None], all_states.astype(jnp.float32), 0.0), axis=0
    )
    carried_mix = jnp.einsum(
        "pbhd,bhde->pbhe", query_rows.astype(jnp.float32), carried, precision=lax.Precision.HIGHEST
    )
    mixed_heads = local_mix + carried_mix
    attended = root_scale(mixed_heads, head_gain.reshape(heads_local, HEAD_DIM), head_eps).astype(
        jnp.bfloat16
    )
    attended = attended.reshape(block_len, batch_size, heads_local * HEAD_DIM)
    own_rows = block_len // head_count
    row_term = jnp.dot(attended, out_weight, preferred_element_type=jnp.float32).astype(
        jnp.bfloat16
    )
    projected = lax.psum_scatter(
        lax.optimization_barrier(row_term).astype(jnp.float32).astype(jnp.bfloat16),
        "head",
        scatter_dimension=0,
        tiled=True,
    ).astype(jnp.float32)
    own_stream = lax.dynamic_slice_in_dim(stream, lax.axis_index("head") * own_rows, own_rows, 0)
    total_rows = own_rows * batch_size
    residual_stream = (own_stream + projected).reshape(total_rows, model_width)
    moe_input = root_scale(residual_stream, moe_gain, norm_eps).astype(jnp.bfloat16)
    capacity = max(2, 3 * total_rows * TOP // (2 * EXPERTS))
    device_count = seq_count * head_count
    both = ("seq", "head")
    halves_local = expert_gate.shape[0]
    device_rank = lax.axis_index("seq") * head_count + lax.axis_index("head")
    routes = jnp.concatenate(
        [
            route_ids.reshape(total_rows, TOP).astype(jnp.float32),
            route_weight.reshape(total_rows, TOP),
        ],
        axis=1,
    )
    routes = lax.all_gather(routes, both, axis=0, tiled=False)
    ids = routes[:, :, :TOP].astype(jnp.int32)
    weights = routes[:, :, TOP:]
    per = max(1, halves_local // 2)
    share = halves_local // per
    own_experts = device_rank * halves_local // 2 + jnp.arange(per, dtype=jnp.int32)
    named = ids[:, None, :, :] == own_experts[None, :, None, None]
    match = jnp.any(named, axis=3)
    gate_weight = jnp.sum(jnp.where(named, weights[:, None], 0.0), axis=3)
    row_index = lax.broadcasted_iota(jnp.int32, (total_rows, total_rows), 0)
    col_index = lax.broadcasted_iota(jnp.int32, (total_rows, total_rows), 1)
    before = (row_index < col_index).astype(jnp.bfloat16)
    slot = jnp.einsum(
        "blt,tu->blu", match.astype(jnp.bfloat16), before, preferred_element_type=jnp.float32
    ).astype(jnp.int32)
    slots = jnp.arange(capacity, dtype=jnp.int32)
    placed = match[:, :, None, :] & (slot[:, :, None, :] == slots[None, None, :, None])
    pick = placed.astype(jnp.bfloat16).reshape(device_count, per * capacity, total_rows)
    blend = jnp.where(placed, gate_weight[:, :, None, :], 0.0).astype(jnp.bfloat16)
    blend = blend.reshape(device_count, per * capacity, total_rows)
    rows = lax.all_gather(moe_input, both, axis=0, tiled=False)
    picked = jnp.einsum("bst,btd->bsd", pick, rows, preferred_element_type=jnp.float32)
    picked = picked.astype(jnp.bfloat16).reshape(device_count, per, capacity, model_width)
    sums = []
    for local in range(per):
        expert_rows = picked[:, local].reshape(device_count * capacity, model_width)
        total = None
        for half in range(share):
            index = local * share + half
            gate_rows = jnp.dot(
                expert_rows, expert_gate[index], preferred_element_type=jnp.float32
            )
            up_rows = jnp.dot(expert_rows, expert_up[index], preferred_element_type=jnp.float32)
            activated = (jax.nn.silu(gate_rows) * up_rows).astype(jnp.bfloat16)
            part = jnp.dot(activated, expert_down[index], preferred_element_type=jnp.float32)
            total = part if total is None else total + part
        sums.append(
            total.astype(jnp.bfloat16).reshape(device_count, 1, capacity, model_width)
        )
    expert_sum = jnp.concatenate(sums, axis=1).reshape(device_count, per * capacity, model_width)
    partial = jnp.einsum("bst,bsd->btd", blend, expert_sum, preferred_element_type=jnp.float32)
    moe_output = lax.psum_scatter(
        partial.astype(jnp.bfloat16), both, scatter_dimension=0, tiled=False
    ).astype(jnp.float32)
    return (
        (residual_stream + moe_output)
        .astype(jnp.bfloat16)
        .reshape(own_rows, batch_size, model_width)
    )


def solution(mesh):
    in_specs = (
        P("seq", None, "head"),
        P(),
        P(None, "head"),
        P(None, "head"),
        P(None, "head"),
        P("head"),
        P("head", None),
        P(),
        P(("seq", "head"), None, None),
        P(("seq", "head"), None, None),
        P(("seq", "head"), None, None),
        P(("seq", "head"), None, None),
        P(("seq", "head"), None, None),
    )
    out_specs = P(("seq", "head"), None, None)
    return jax.shard_map(body, mesh=mesh, in_specs=in_specs, out_specs=out_specs, check_vma=False)
```

time: 842 us -> 567 us (0.67)
  waiting for transfers between devices: 510 us -> 370 us
  local copies, waits for them, and re-layouts: 119 us -> 13.1 us
  other arithmetic: 86.4 us -> 17.4 us
  starting transfers between devices: 55.8 us -> 0.17 us
  matrix products: 50.9 us -> 106 us
  blocking collectives: 0 us -> 42.4 us
    all_to_all x2 -> x0, waiting for transfers between devices: 415 us -> none  [the longest x1 275 us: body(): lax.all_to_all(sending, ('seq', 'head'), split_axis=0, concat_axis=1, til...]
    reduce_scatter x0 -> x1, waiting for transfers between devices: none -> 181 us  [body(): lax.psum_scatter(partial.astype(jnp.bfloat16), both, scatter_dimension=0,...]
    all_gather x0 -> x2, waiting for transfers between devices: none -> 138 us  [the longest x1 71.2 us: body(): rows = lax.all_gather(moe_input, both, axis=0, tiled=False)]
    ppermute x7 -> x0, waiting for transfers between devices: 59.5 us -> none  [passed_along(): return lax.ppermute(x, axis, pairs)]
    dot_general x2 -> x11, matrix products: 31.9 us -> 87.1 us  [the longest x4 50.1 us: body(): jnp.dot(activated, expert_down[index], preferred_element_type=jnp.float32)]
    all_gather x0 -> x1, blocking collectives: none -> 42.4 us  [body(): routes = lax.all_gather(routes, both, axis=0, tiled=False)]
    ppermute x7 -> x0, starting transfers between devices: 38.7 us -> none  [passed_along(): return lax.ppermute(x, axis, pairs)]
    slice x4 -> x2, local copies, waits for them, and re-layouts: 19 us -> 0.66 us  [the longest x1 0.58 us: body(): expert_rows = picked[:, local].reshape(device_count * capacity, model_width)]
  transfers between devices with their start and end apart: 11 -> 5, of which waited for: 11 -> 5; matrix products, arithmetic and copies ran while one was open for 3% -> 2% of each run, Pallas kernels for 0% -> 0%
where the time goes in v1:
time: 567 us; the launch traced here: 562 us
  waiting for transfers between devices  370 us (65%)
  matrix products  106 us (19%)
  blocking collectives  42.4 us (7%)
  other arithmetic  17.4 us (3%)
  between operations  13.7 us (2%)
  local copies, waits for them, and re-layouts  13.1 us (2%)
    reduce_scatter x1, waiting for transfers between devices, body(): lax.psum_scatter(partial.astype(jnp.bfloat16), both, scatter_dimension=0,...  181 us
    all_gather x1, waiting for transfers between devices, body(): rows = lax.all_gather(moe_input, both, axis=0, tiled=False)  71.2 us
    all_gather x1, waiting for transfers between devices, body(): lax.all_gather(local_state.astype(jnp.bfloat16), 'seq', axis=0, tiled=False)  66.3 us
    dot_general x4, matrix products, body(): jnp.dot(activated, expert_down[index], preferred_element_type=jnp.float32)  50.1 us
    all_gather x1, blocking collectives, body(): routes = lax.all_gather(routes, both, axis=0, tiled=False)  42.4 us
    reduce_scatter x1, waiting for transfers between devices, body(): lax.psum_scatter(lax.optimization_barrier(row_term).astype(jnp.float32).a...  25.8 us
    all_gather x1, waiting for transfers between devices, body(): gathered = lax.all_gather(tokens, 'head', axis=2, tiled=True)  24.9 us
    dot_general x4, matrix products, body(): jnp.dot(expert_rows, expert_gate[index], preferred_element_type=jnp.float32)  15.7 us
  transfers between devices with their start and end apart: 5, of which 5 were waited for; matrix products, arithmetic and copies ran while one was open for 2% of the time, Pallas kernels for 0%

profile of v1, /device:TPU:0, one launch (start us, length us, event | category | flops | bytes accessed | tf_op | source)
XLA Modules:
  0.0 562.5 jit_solution(17865724625917707131)
XLA Ops:
  6.5 2.1 copy.60
  8.6 0.0 all-gather.6.cloned.1.call-update
  8.6 0.0 all-gather.10.cloned.1.call-start
  8.7 0.7 convert_element_type.117
  9.4 24.9 %all-gather.6.cloned.1.call-done = bf16[128,4,2048]{2,0,1:T(8,128)(2,1)} async-done(((bf16[128,4,512]{2,0,1:T(8,128)(2,1)}), bf16[128,4,2048]{2,0,1:T(8,128)(2,1)}) %all-gather.6.cloned.1.call-update) | async-done | bytes 2097168 | tf_op jit(solution)/shard_map/all_gather | solution.py:40
  34.2 2.1 multiply_reduce_fusion
  36.3 3.7 multiply_convert_fusion.10
  40.0 0.3 copy.84
  40.3 3.5 fusion.56
  43.8 1.1 convolution_convert_fusion.3
  44.9 0.0 all-gather.10.cloned.1.call-update
  44.9 0.0 reduce-scatter.3.cloned.1.call-start
  45.0 4.5 fusion.76
  49.5 2.7 fusion.55
  52.2 66.3 %all-gather.10.cloned.1.call-done = bf16[32,4,128,128]{3,2,1,0:T(8,128)(2,1)} async-done(((bf16[4,4,128,128]{3,2,1,0:T(8,128)(2,1)}), bf16[32,4,128,128]{3,2,1,0:T(8,128)(2,1)}) %all-gather.10.cloned.1.call-update) | async-done | bytes 4194320 | tf_op jit(solution)/shard_map/all_gather | solution.py:64
  118.5 3.3 fusion
  121.8 1.1 multiply_reduce_fusion.2
  122.9 0.2 multiply_convert_fusion.9
  123.1 2.6 convolution_convert_fusion.2
  125.7 0.0 reduce-scatter.3.cloned.1.call-update
  125.7 0.0 all-gather.8.cloned.1.call-start
  125.8 1.5 copy-done.2
  127.3 2.5 convert_element_type.116
  129.8 25.8 %reduce-scatter.3.cloned.1.call-done = bf16[32,4,2048]{2,0,1:T(8,128)(2,1)} async-done(((bf16[128,4,2048]{2,0,1:T(8,128)(2,1)}), bf16[32,4,2048]{2,0,1:T(8,128)(2,1)}) %reduce-scatter.3.cloned.1.call-update) | async-done | bytes 524304 | tf_op jit(solution)/shard_map/reduce_scatter | solution.py:81
  155.6 1.6 multiply_reduce_fusion.1
  157.2 0.7 copy.77
  157.9 0.4 reshape.162
  158.3 0.1 copy.78
  158.4 0.1 rsqrt.30
  158.5 1.0 multiply_convert_fusion.8
  159.4 0.0 all-gather.8.cloned.1.call-update
  159.5 0.0 reduce-scatter.5.cloned.1.call-start
  159.6 0.1 copy.69
  159.7 0.1 copy.70
  159.9 42.4 %all-gather.1 = f32[4096,16]{0,1:T(8,128)S(1)} all-gather(f32[128,16]{0,1:T(8,128)S(1)} %pad_maximum_fusion.1), channel_id=3, replica_groups=mesh['seq'=8,'head'=4] {'seq','head'}, dimensions={0}, use_global_device_ids=true | all-gather | bytes 270336 | tf_op jit(solution)/shard_map/all_gather | solution.py:103
  202.3 0.1 copy.87
  202.3 0.1 copy.73
  202.4 0.2 compare_reduce_fusion
  202.6 0.1 convolution_convert_fusion.4
  202.8 0.1 eq.40
  202.9 0.1 copy.76
  203.0 0.2 fusion.73
  203.2 0.2 fusion.93
  203.3 0.2 fusion.68
  203.6 71.2 %all-gather.8.cloned.1.call-done = bf16[32,128,2048]{2,1,0:T(8,128)(2,1)} async-done(((bf16[1,128,2048]{2,1,0:T(8,128)(2,1)}), bf16[32,128,2048]{2,1,0:T(8,128)(2,1)}) %all-gather.8.cloned.1.call-update) | async-done | bytes 16777232 | tf_op jit(solution)/shard_map/all_gather | solution.py:123
  274.8 8.1 %convolution_convert_fusion.1 = bf16[32,48,2048]{2,1,0:T(8,128)(2,1)S(1)} fusion(pred[32,48,128]{2,1,0:T(8,128)(4,1)S(1)} %fusion.73, bf16[32,128,2048]{2,1,0:T(8,128)(2,1)} %all-gather.8.cloned.1.call-done), kind=kOutput, calls=%fused_computation.6 | convolution fusion | flops 808452096 | bytes 23265280 | tf_op jit(solution)/shard_map/bst,btd->bsd/dot_general | solution.py:124
  282.8 0.6 fusion.102
  283.4 0.0 slice-start
  283.5 6.2 %fusion.21 = f32[768,512]{1,0:T(8,128)} fusion(bf16[768,2048]{1,0:T(8,128)(2,1)S(1)} %bitcast.154, bf16[4,2048,512]{2,1,0:T(8,128)(2,1)} %param.23), kind=kOutput, calls=%fused_computation.30 | convolution fusion | flops 1610612736 | bytes 6815744 | tf_op jit(solution)/shard_map/dot_general | solution.py:132
  289.7 4.7 fusion.15
  294.4 3.0 fusion.10
  297.4 1.8 fusion.4
  299.2 9.8 %fusion.17 = f32[768,2048]{1,0:T(8,128)} fusion(bf16[4,512,2048]{2,1,0:T(8,128)(2,1)} %param.25, f32[768,512]{1,0:T(8,128)} %fusion.21, bf16[768,2048]{1,0:T(8,128)(2,1)} %bitcast.156, bf16[4,2048,512]{2,1,0:T(8,128)(2,1)} %param.24), kind=kOutput, calls=%fused_computation.26 | convolution fusion | flops 3223584768 | bytes 15204352 | tf_op jit(solution)/shard_map/dot_general | solution.py:137
  309.0 19.6 %fusion.6 = f32[768,2048]{1,0:T(8,128)} fusion(bf16[4,512,2048]{2,1,0:T(8,128)(2,1)} %param.25, f32[768,512]{1,0:T(8,128)} %fusion.10, bf16[768,2048]{1,0:T(8,128)(2,1)} %bitcast.152, bf16[4,2048,512]{2,1,0:T(8,128)(2,1)} %param.24), kind=kOutput, calls=%fused_computation.15 | convolution fusion | flops 3223584768 | bytes 15204352 | tf_op jit(solution)/shard_map/dot_general | solution.py:137
  328.6 10.6 %add_convert_fusion.1 = bf16[768,2048]{1,0:T(8,128)(2,1)} fusion(f32[768,2048]{1,0:T(8,128)} %fusion.17, bf16[4,512,2048]{2,1,0:T(8,128)(2,1)} %param.25, f32[768,512]{1,0:T(8,128)} %fusion.15, bf16[768,2048]{1,0:T(8,128)(2,1)} %bitcast.157, bf16[4,2048,512]{2,1,0:T(8,128)(2,1)} %param.24), kind=kOutput, calls=%fused_computation.5 | convolution fusion | flops 3226730496 | bytes 18350080 | tf_op jit(solution)/shard_map/dot_general | solution.py:137
  339.2 10.1 %add_convert_fusion = bf16[768,2048]{1,0:T(8,128)(2,1)} fusion(f32[768,2048]{1,0:T(8,128)} %fusion.6, bf16[4,512,2048]{2,1,0:T(8,128)(2,1)} %param.25, f32[768,512]{1,0:T(8,128)S(1)} %fusion.4, bf16[768,2048]{1,0:T(8,128)(2,1)} %bitcast.153, bf16[4,2048,512]{2,1,0:T(8,128)(2,1)} %param.24), kind=kOutput, calls=%fused_computation.4 | convolution fusion | flops 3226730496 | bytes 18350080 | tf_op jit(solution)/shard_map/dot_general | solution.py:137
  349.3 3.4 pad_maximum_fusion
  352.7 3.2 copy.79
  356.0 13.1 %convolution_convert_fusion = bf16[32,128,2048]{2,1,0:T(8,128)(2,1)} fusion(bf16[32,48,128]{2,1,0:T(8,128)(2,1)S(1)} %fusion.68, bf16[32,48,2048]{2,1,0:T(8,128)(2,1)} %bitcast.146), kind=kOutput, calls=%fused_computation | convolution fusion | flops 813694976 | bytes 23461888 | tf_op jit(solution)/shard_map/bst,bsd->btd/dot_general | solution.py:143
  369.0 0.0 reduce-scatter.5.cloned.1.call-update
  369.1 181.3 %reduce-scatter.5.cloned.1.call-done = bf16[1,128,2048]{2,1,0:T(8,128)(2,1)} async-done(((bf16[32,128,2048]{2,1,0:T(8,128)(2,1)}), bf16[1,128,2048]{2,1,0:T(8,128)(2,1)}) %reduce-scatter.5.cloned.1.call-update) | async-done | bytes 524304 | tf_op jit(solution)/shard_map/reduce_scatter | solution.py:144
  550.4 2.3 reshape.168
  552.7 1.8 fusion.63
  554.5 1.2 copy.81
  (41 shorter events, 0.3 us)
Async XLA Ops:
  6.5 116.5 %copy-start = (bf16[512,2048]{1,0:T(8,128)(2,1)S(1)}, bf16[512,2048]{1,0:T(8,128)(2,1)}, u32[]{:S(2)}) copy-start(bf16[512,2048]{1,0:T(8,128)(2,1)} %param.19) | copy-start | bytes 6291460
  6.5 27.7 %all-gather.6.cloned.1.call-start = ((), (), s32[]{:S(2)}) async-start(), calls=%async_computation.2 | async-start | bytes 2621440 | tf_op jit(solution)/shard_map/all_gather | solution.py:40
  8.6 109.9 %all-gather.10.cloned.1.call-start = ((), (), s32[]{:S(2)}) async-start(), calls=%async_computation.6 | async-start | bytes 4718592 | tf_op jit(solution)/shard_map/all_gather | solution.py:64
  40.3 4.8 copy-start.10
  44.9 110.7 %reduce-scatter.3.cloned.1.call-start = ((), (), s32[]{:S(2)}) async-start(), calls=%async_computation.3 | async-start | bytes 2621440 | tf_op jit(solution)/shard_map/reduce_scatter | solution.py:81
  52.2 69.6 %copy-start.3 = (f32[4,4,128,128]{3,2,1,0:T(8,128)S(1)}, f32[4,4,128,128]{3,2,1,0:T(8,128)}, u32[]{:S(2)}) copy-start(f32[4,4,128,128]{3,2,1,0:T(8,128)} %fusion.55) | copy-start | bytes 3145732
  118.5 3.3 copy-start.6
  123.1 2.7 copy-start.9
  125.7 1.6 copy-start.2
  125.7 149.0 %all-gather.8.cloned.1.call-start = ((), (), s32[]{:S(2)}) async-start(), calls=%async_computation.4 | async-start | bytes 17301504 | tf_op jit(solution)/shard_map/all_gather | solution.py:123
  157.2 2.3 copy-start.8
  157.2 2.5 copy-start.7
  159.5 390.9 %reduce-scatter.5.cloned.1.call-start = ((), (), s32[]{:S(2)}) async-start(), calls=%async_computation.5 | async-start | bytes 17301504 | tf_op jit(solution)/shard_map/reduce_scatter | solution.py:144
  283.4 6.3 %copy-start.5 = (bf16[32,1,24,2048]{3,2,1,0:T(8,128)(2,1)}, bf16[32,1,24,2048]{3,2,1,0:T(8,128)(2,1)S(1)}, u32[]{:S(2)}) copy-start(bf16[32,1,24,2048]{3,2,1,0:T(8,128)(2,1)S(1)} %get-tuple-element.7) | copy-start | bytes 9437188
  283.4 14.0 %copy-start.4 = (bf16[32,1,24,2048]{3,2,1,0:T(8,128)(2,1)}, bf16[32,1,24,2048]{3,2,1,0:T(8,128)(2,1)S(1)}, u32[]{:S(2)}) copy-start(bf16[32,1,24,2048]{3,2,1,0:T(8,128)(2,1)S(1)} %get-tuple-element.8) | copy-start | bytes 9437188
  283.4 11.0 %slice-start = ((s8[8388608]{0:T(1024)(128)(4,1)}), s8[4194304]{0:T(1024)(128)(4,1)S(1)}, s32[]{:S(2)}) async-start(s8[8388608]{0:T(1024)(128)(4,1)} %bitcast.165), calls=%async_computation.7 | async-start | bytes 8388608
  289.7 4.7 slice-start.1
  369.1 186.7 %copy-start.1 = (bf16[512,2048]{1,0:T(8,128)(2,1)S(1)}, bf16[512,2048]{1,0:T(8,128)(2,1)}, u32[]{:S(2)}) copy-start(bf16[512,2048]{1,0:T(8,128)(2,1)} %param.19) | copy-start | bytes 6291460
Sparse Core Ops, SparseCore 0:
  8.9 25.2 all-gather.5
  45.1 73.3 all-gather.9
  125.9 29.7 reduce-scatter.2
  159.6 115.1 all-gather.7
  369.2 181.1 reduce-scatter.4

commit v2 on v1

--- a/solution.py
+++ b/solution.py
@@ -39,6 +39,12 @@
     seq_count = lax.axis_size("seq")
     gathered = lax.all_gather(tokens, "head", axis=2, tiled=True)
     block_len, batch_size, model_width = gathered.shape
+    both = ("seq", "head")
+    own_routes = jnp.concatenate(
+        [route_ids.reshape(-1, TOP).astype(jnp.float32), route_weight.reshape(-1, TOP)], axis=1
+    )
+    routes = lax.all_gather(own_routes, both, axis=0, tiled=False)
+    gathered, routes = lax.optimization_barrier((gathered, routes))
     stream = gathered.astype(jnp.float32)
     normed = root_scale(stream, attn_gain, norm_eps).astype(jnp.bfloat16)
     heads_local = query_weight.shape[1] // HEAD_DIM
@@ -61,11 +67,15 @@
         "sbhd,sbhe->bhde", key_rows, value_rows, preferred_element_type=jnp.float32
     )
 
-    all_states = lax.all_gather(local_state.astype(jnp.bfloat16), "seq", axis=0, tiled=False)
-    earlier = jnp.arange(seq_count, dtype=jnp.int32) < lax.axis_index("seq")
-    carried = jnp.sum(
-        jnp.where(earlier[:, None, None, None, None], all_states.astype(jnp.float32), 0.0), axis=0
-    )
+    shares = local_state.astype(jnp.bfloat16).reshape(seq_count, -1, HEAD_DIM)
+    shares = lax.all_to_all(shares, "seq", split_axis=0, concat_axis=0, tiled=True)
+    running = jnp.zeros(shares.shape[1:], jnp.float32)
+    prefixes = []
+    for block in range(seq_count):
+        prefixes.append(running.astype(jnp.bfloat16))
+        running = running + shares[block].astype(jnp.float32)
+    carried = lax.all_to_all(jnp.stack(prefixes), "seq", split_axis=0, concat_axis=0, tiled=True)
+    carried = carried.reshape(local_state.shape).astype(jnp.float32)
     carried_mix = jnp.einsum(
         "pbhd,bhde->pbhe", query_rows.astype(jnp.float32), carried, precision=lax.Precision.HIGHEST
     )
@@ -90,60 +100,94 @@
     moe_input = root_scale(residual_stream, moe_gain, norm_eps).astype(jnp.bfloat16)
     capacity = max(2, 3 * total_rows * TOP // (2 * EXPERTS))
     device_count = seq_count * head_count
-    both = ("seq", "head")
     halves_local = expert_gate.shape[0]
     device_rank = lax.axis_index("seq") * head_count + lax.axis_index("head")
-    routes = jnp.concatenate(
-        [
-            route_ids.reshape(total_rows, TOP).astype(jnp.float32),
-            route_weight.reshape(total_rows, TOP),
-        ],
-        axis=1,
-    )
-    routes = lax.all_gather(routes, both, axis=0, tiled=False)
     ids = routes[:, :, :TOP].astype(jnp.int32)
     weights = routes[:, :, TOP:]
     per = max(1, halves_local // 2)
     share = halves_local // per
     own_experts = device_rank * halves_local // 2 + jnp.arange(per, dtype=jnp.int32)
-    named = ids[:, None, :, :] == own_experts[None, :, None, None]
-    match = jnp.any(named, axis=3)
-    gate_weight = jnp.sum(jnp.where(named, weights[:, None], 0.0), axis=3)
     row_index = lax.broadcasted_iota(jnp.int32, (total_rows, total_rows), 0)
     col_index = lax.broadcasted_iota(jnp.int32, (total_rows, total_rows), 1)
     before = (row_index < col_index).astype(jnp.bfloat16)
-    slot = jnp.einsum(
-        "blt,tu->blu", match.astype(jnp.bfloat16), before, preferred_element_type=jnp.float32
-    ).astype(jnp.int32)
     slots = jnp.arange(capacity, dtype=jnp.int32)
-    placed = match[:, :, None, :] & (slot[:, :, None, :] == slots[None, None, :, None])
-    pick = placed.astype(jnp.bfloat16).reshape(device_count, per * capacity, total_rows)
-    blend = jnp.where(placed, gate_weight[:, :, None, :], 0.0).astype(jnp.bfloat16)
-    blend = blend.reshape(device_count, per * capacity, total_rows)
-    rows = lax.all_gather(moe_input, both, axis=0, tiled=False)
-    picked = jnp.einsum("bst,btd->bsd", pick, rows, preferred_element_type=jnp.float32)
-    picked = picked.astype(jnp.bfloat16).reshape(device_count, per, capacity, model_width)
-    sums = []
+
+    def tables(ids, weights, experts):
+        named = ids[:, None, :, :] == experts[:, :, None, None]
+        match = jnp.any(named, axis=3)
+        gate_weight = jnp.sum(jnp.where(named, weights[:, None], 0.0), axis=3)
+        slot = jnp.einsum(
+            "blt,tu->blu", match.astype(jnp.bfloat16), before, preferred_element_type=jnp.float32
+        ).astype(jnp.int32)
+        placed = match[:, :, None, :] & (slot[:, :, None, :] == slots[None, None, :, None])
+        blend = jnp.where(placed, gate_weight[:, :, None, :], 0.0).astype(jnp.bfloat16)
+        shape = (device_count, per * capacity, total_rows)
+        return placed.astype(jnp.bfloat16).reshape(shape), blend.reshape(shape)
+
+    pick, blend = tables(ids, weights, own_experts[None])
+    all_experts = (
+        jnp.arange(device_count, dtype=jnp.int32)[:, None] * halves_local // 2
+        + jnp.arange(per, dtype=jnp.int32)[None]
+    )
+    own_pick, own_blend = tables(
+        own_routes[None, :, :TOP].astype(jnp.int32), own_routes[None, :, TOP:], all_experts
+    )
+    cut_in = model_width * 5 // 8
+    cut_out = model_width // 2
+    sending = jnp.einsum(
+        "bst,td->bsd", own_pick, moe_input[:, cut_in:], preferred_element_type=jnp.float32
+    ).astype(jnp.bfloat16)
+    rows = lax.all_gather(moe_input[:, :cut_in], both, axis=0, tiled=False)
+    received = lax.all_to_all(sending, both, split_axis=0, concat_axis=0, tiled=True)
+    picked = jnp.einsum(
+        "bst,btd->bsd", pick, rows, preferred_element_type=jnp.float32
+    ).astype(jnp.bfloat16)
+    picked = jnp.concatenate([picked, received], axis=2)
+    picked = picked.reshape(device_count, per, capacity, model_width)
+    hidden = []
     for local in range(per):
         expert_rows = picked[:, local].reshape(device_count * capacity, model_width)
-        total = None
         for half in range(share):
             index = local * share + half
             gate_rows = jnp.dot(
                 expert_rows, expert_gate[index], preferred_element_type=jnp.float32
             )
             up_rows = jnp.dot(expert_rows, expert_up[index], preferred_element_type=jnp.float32)
-            activated = (jax.nn.silu(gate_rows) * up_rows).astype(jnp.bfloat16)
-            part = jnp.dot(activated, expert_down[index], preferred_element_type=jnp.float32)
-            total = part if total is None else total + part
-        sums.append(
-            total.astype(jnp.bfloat16).reshape(device_count, 1, capacity, model_width)
-        )
-    expert_sum = jnp.concatenate(sums, axis=1).reshape(device_count, per * capacity, model_width)
-    partial = jnp.einsum("bst,bsd->btd", blend, expert_sum, preferred_element_type=jnp.float32)
-    moe_output = lax.psum_scatter(
-        partial.astype(jnp.bfloat16), both, scatter_dimension=0, tiled=False
-    ).astype(jnp.float32)
+            hidden.append((jax.nn.silu(gate_rows) * up_rows).astype(jnp.bfloat16))
+
+    def summed(hidden, low, high):
+        sums = []
+        for local in range(per):
+            total = 0.0
+            for index in range(local * share, (local + 1) * share):
+                total = total + jnp.dot(
+                    hidden[index],
+                    expert_down[index, :, low:high],
+                    preferred_element_type=jnp.float32,
+                )
+            sums.append(
+                total.astype(jnp.bfloat16).reshape(device_count, 1, capacity, high - low)
+            )
+        return jnp.concatenate(sums, axis=1).reshape(device_count, per * capacity, high - low)
+
+    partial = jnp.einsum(
+        "bst,bsd->btd",
+        blend,
+        summed(hidden, 0, cut_out),
+        preferred_element_type=jnp.float32,
+    ).astype(jnp.bfloat16)
+    partial, hidden = lax.optimization_barrier((partial, hidden))
+    lower = lax.psum_scatter(partial, both, scatter_dimension=0, tiled=False)
+    returned = lax.all_to_all(
+        summed(hidden, cut_out, model_width), both, split_axis=0, concat_axis=0, tiled=True
+    )
+    upper = jnp.einsum(
+        "kt,kd->td",
+        own_blend.reshape(-1, total_rows),
+        returned.reshape(-1, model_width - cut_out),
+        preferred_element_type=jnp.float32,
+    )
+    moe_output = jnp.concatenate([lower.astype(jnp.float32), upper], axis=1)
     return (
         (residual_stream + moe_output)
         .astype(jnp.bfloat16)

time: 567 us -> 500 us (0.88)
  waiting for transfers between devices: 370 us -> 305 us
  matrix products: 106 us -> 78.3 us
  starting transfers between devices: 0.17 us -> 16.3 us
    reduce_scatter x1, waiting for transfers between devices: 181 us -> 66.5 us  [body(): lower = lax.psum_scatter(partial, both, scatter_dimension=0, tiled=False)]
    all_to_all x0 -> x4, waiting for transfers between devices: none -> 108 us  [the longest x1 85.9 us: body(): lax.all_to_all(summed(hidden, cut_out, model_width), both, split_axis=0,...]
    all_gather x2 -> x1, waiting for transfers between devices: 138 us -> 105 us  [body(): rows = lax.all_gather(moe_input[:, :cut_in], both, axis=0, tiled=False)]
    all_gather x1, waiting for transfers between devices: 24.9 us -> 0.01 us  [body(): gathered = lax.all_gather(tokens, 'head', axis=2, tiled=True)]
    dot_general x6 -> x17, matrix products: 63.3 us -> 41.3 us  [the longest x4 16.9 us: body(): jnp.dot(expert_rows, expert_up[index], preferred_element_type=jnp.float32)]
    all_to_all x0 -> x4, starting transfers between devices: none -> 15.9 us  [the longest x1 4.72 us: body(): lax.all_to_all(sending, both, split_axis=0, concat_axis=0, tiled=True)]
  transfers between devices with their start and end apart: 5 -> 8, of which waited for: 5 -> 6; matrix products, arithmetic and copies ran while one was open for 2% -> 8% of each run, Pallas kernels for 0% -> 0%
where the time goes in v2:
time: 500 us; the launch traced here: 495 us
  waiting for transfers between devices  305 us (61%)
  matrix products  78.3 us (16%)
  blocking collectives  44.1 us (9%)
  other arithmetic  20.6 us (4%)
  starting transfers between devices  16.3 us (3%)
  local copies, waits for them, and re-layouts  16.2 us (3%)
  between operations  14 us (3%)
    all_gather x1, waiting for transfers between devices, body(): rows = lax.all_gather(moe_input[:, :cut_in], both, axis=0, tiled=False)  105 us
    all_to_all x1, waiting for transfers between devices, body(): lax.all_to_all(summed(hidden, cut_out, model_width), both, split_axis=0,...  85.9 us
    reduce_scatter x1, waiting for transfers between devices, body(): lower = lax.psum_scatter(partial, both, scatter_dimension=0, tiled=False)  66.5 us
    all_gather x1, blocking collectives, body(): routes = lax.all_gather(own_routes, both, axis=0, tiled=False)  44.1 us
    reduce_scatter x1, waiting for transfers between devices, body(): lax.psum_scatter(lax.optimization_barrier(row_term).astype(jnp.float32).a...  25.6 us
    dot_general x4, matrix products, body(): jnp.dot(expert_rows, expert_up[index], preferred_element_type=jnp.float32)  16.9 us
    all_to_all x1, waiting for transfers between devices, body(): lax.all_to_all(shares, 'seq', split_axis=0, concat_axis=0, tiled=True)  14.6 us
    dot_general x8, matrix products, summed(): jnp.dot(hidden[index], expert_down[index, :, low:high], preferred_element...  12.9 us
  transfers between devices with their start and end apart: 8, of which 6 were waited for; matrix products, arithmetic and copies ran while one was open for 8% of the time, Pallas kernels for 0%

profile of v2, /device:TPU:0, one launch (start us, length us, event | category | flops | bytes accessed | tf_op | source)
XLA Modules:
  0.0 494.7 jit_solution(17023678208614461958)
XLA Ops:
  6.5 2.1 copy.99
  8.6 0.7 convert_element_type.214
  9.5 0.8 copy.101
  10.4 44.1 %all-gather = f32[4096,16]{0,1:T(8,128)S(1)} all-gather(f32[128,16]{0,1:T(8,128)S(1)} %pad_maximum_fusion.3), channel_id=2, replica_groups=mesh['seq'=8,'head'=4] {'seq','head'}, dimensions={0}, use_global_device_ids=true | all-gather | bytes 270336 | tf_op jit(solution)/shard_map/all_gather | solution.py:46
  54.6 0.7 convert_element_type.217
  55.3 2.1 multiply_reduce_fusion
  57.4 3.7 fusion.45
  61.1 2.2 multiply_convert_fusion.10
  63.3 1.3 copy.131
  64.7 1.1 convolution_convert_fusion.4
  65.8 3.5 all-to-all-start
  69.3 0.6 broadcast_dynamic-update-slice_fusion
  69.9 14.6 %all-to-all-done = bf16[8,256,128]{2,1,0:T(8,128)(2,1)S(1)} async-done(((bf16[8,256,128]{2,1,0:T(8,128)(2,1)}), bf16[8,256,128]{2,1,0:T(8,128)(2,1)S(1)}, u32[]{:S(2)}, u32[]{:S(2)}) %all-to-all-start) | async-done | bytes 524320 | tf_op jit(solution)/shard_map/all_to_all | solution.py:71
  84.5 0.6 slice_dynamic-update-slice_fusion
  85.1 0.6 fusion.102
  85.7 0.6 convert_dynamic-update-slice_fusion.1
  86.4 0.7 fusion.101
  87.0 0.7 convert_dynamic-update-slice_fusion
  87.7 0.6 fusion.100
  88.3 0.7 fusion.103
  89.0 4.1 all-to-all-start.1
  93.2 4.5 fusion.76
  97.7 2.6 fusion.44
  100.4 7.2 %all-to-all-done.1 = bf16[8,256,128]{2,1,0:T(8,128)(2,1)} async-done(((bf16[8,256,128]{2,1,0:T(8,128)(2,1)}), bf16[8,256,128]{2,1,0:T(8,128)(2,1)}, u32[]{:S(2)}, u32[]{:S(2)}) %all-to-all-start.1) | async-done | bytes 524320 | tf_op jit(solution)/shard_map/all_to_all | solution.py:77
  107.6 2.1 multiply_reduce_fusion.2
  109.9 2.6 convolution_convert_fusion.2
  112.7 1.5 copy-done.3
  114.1 2.5 convert_element_type.216
  116.6 25.6 %reduce-scatter.3.cloned.1.call-done = bf16[32,4,2048]{2,0,1:T(8,128)(2,1)} async-done(((bf16[128,4,2048]{2,0,1:T(8,128)(2,1)}), bf16[32,4,2048]{2,0,1:T(8,128)(2,1)}) %reduce-scatter.3.cloned.1.call-update) | async-done | bytes 524304 | tf_op jit(solution)/shard_map/reduce_scatter | solution.py:91
  142.3 1.6 multiply_reduce_fusion.1
  143.9 0.7 copy.116
  145.3 0.8 slice.123
  147.4 2.2 convolution_convert_fusion.3
  149.6 4.7 all-to-all-start.2
  155.2 105.3 %all-gather.7.cloned.1.call-done = bf16[4096,1280]{1,0:T(8,128)(2,1)} async-done(((bf16[128,1280]{1,0:T(8,128)(2,1)}), bf16[4096,1280]{1,0:T(8,128)(2,1)}) %all-gather.7.cloned.1.call-update) | async-done | bytes 10485776 | tf_op jit(solution)/shard_map/all_gather | solution.py:140
  260.5 7.5 %convolution_convert_fusion.1 = bf16[32,48,1280]{2,1,0:T(8,128)(2,1)} fusion(pred[32,48,128]{2,1,0:T(8,128)(4,1)S(1)} %get-tuple-element.27, bf16[32,128,1280]{2,1,0:T(8,128)(2,1)} %bitcast.193), kind=kOutput, calls=%fused_computation.2 | convolution fusion | flops 505282560 | bytes 14614528 | tf_op jit(solution)/shard_map/bst,btd->bsd/dot_general | solution.py:142
  267.9 3.6 pad_maximum_fusion
  271.6 0.8 fusion.110
  272.4 3.5 fusion.10
  275.9 3.5 fusion.14
  279.5 1.8 fusion.2
  281.3 1.8 fusion.6
  283.6 1.9 multiply_convert_fusion.3
  285.5 1.9 multiply_convert_fusion.4
  287.5 1.9 multiply_convert_fusion.1
  289.5 11.0 %multiply_convert_fusion.2 = bf16[768,512]{1,0:T(8,128)(2,1)S(1)} fusion(f32[768,512]{1,0:T(8,128)S(1)} %fusion.6, bf16[768,2048]{1,0:T(8,128)(2,1)S(1)} %bitcast.208, bf16[4,2048,512]{2,1,0:T(8,128)(2,1)S(1)} %bitcast.226), kind=kOutput, calls=%fused_computation.45 | convolution fusion | flops 1612972032 | bytes 7602176 | tf_op jit(solution)/shard_map/dot_general | solution.py:155
  300.6 1.0 fusion.59
  301.5 1.0 fusion.56
  302.5 1.0 add_convert_fusion.3
  303.5 1.0 add_convert_fusion.2
  305.3 5.7 %convolution_convert_fusion = bf16[32,128,1024]{2,1,0:T(8,128)(2,1)} fusion(bf16[32,48,128]{2,1,0:T(8,128)(2,1)S(1)} %fusion.70, bf16[32,48,1024]{2,1,0:T(8,128)(2,1)S(1)} %bitcast.196), kind=kOutput, calls=%fused_computation | convolution fusion | flops 406847488 | bytes 11927552 | tf_op jit(solution)/shard_map/bst,bsd->btd/dot_general | solution.py:173
  310.9 2.2 fusion.53
  313.2 2.3 fusion.50
  315.5 2.3 add_convert_fusion.1
  317.8 2.2 add_convert_fusion
  320.0 2.0 pad_maximum_fusion.2
  322.0 3.5 all-to-all-start.3
  326.4 85.9 %all-to-all-done.3 = bf16[32,48,1024]{2,1,0:T(8,128)(2,1)} async-done(((bf16[32,48,1024]{2,1,0:T(8,128)(2,1)}), bf16[32,48,1024]{2,1,0:T(8,128)(2,1)}, u32[]{:S(2)}, u32[]{:S(2)}) %all-to-all-start.3) | async-done | bytes 3145760 | tf_op jit(solution)/shard_map/all_to_all | solution.py:181
  412.3 3.4 fusion.93
  415.8 66.5 %reduce-scatter.5.cloned.1.call-done = bf16[1,128,1024]{2,1,0:T(8,128)(2,1)} async-done(((bf16[32,128,1024]{2,1,0:T(8,128)(2,1)}), bf16[1,128,1024]{2,1,0:T(8,128)(2,1)}) %reduce-scatter.5.cloned.1.call-update) | async-done | bytes 262160 | tf_op jit(solution)/shard_map/reduce_scatter | solution.py:180
  482.3 1.9 reshape.224
  484.2 1.3 copy.127
  485.6 1.2 fusion.48
  486.8 1.2 copy.128
  (97 shorter events, 5.6 us)
Async XLA Ops:
  6.5 103.4 %copy-start = (bf16[512,2048]{1,0:T(8,128)(2,1)S(1)}, bf16[512,2048]{1,0:T(8,128)(2,1)}, u32[]{:S(2)}) copy-start(bf16[512,2048]{1,0:T(8,128)(2,1)} %param.19) | copy-start | bytes 6291460
  6.5 48.7 %all-gather.5.cloned.1.call-start = ((), (), s32[]{:S(2)}) async-start(), calls=%async_computation.6 | async-start | bytes 2621440 | tf_op jit(solution)/shard_map/all_gather | solution.py:40
  57.4 3.7 copy-start.2
  57.4 3.7 copy-start.12
  61.1 3.6 copy-start.8
  63.3 6.6 %copy-start.11 = (bf16[512]{0:T(512)(128)(2,1)S(1)}, bf16[512]{0:T(512)(128)(2,1)}, u32[]{:S(2)}) copy-start(bf16[512]{0:T(512)(128)(2,1)} %param.18) | copy-start | bytes 3076
  65.8 18.7 %all-to-all-start = ((bf16[8,256,128]{2,1,0:T(8,128)(2,1)}), bf16[8,256,128]{2,1,0:T(8,128)(2,1)S(1)}, u32[]{:S(2)}, u32[]{:S(2)}) async-start(bf16[8,256,128]{2,1,0:T(8,128)(2,1)} %bitcast.213), calls=%async_computation | async-start | bytes 1048576 | tf_op jit(solution)/shard_map/all_to_all | solution.py:71
  89.0 18.6 %all-to-all-start.1 = ((bf16[8,256,128]{2,1,0:T(8,128)(2,1)}), bf16[8,256,128]{2,1,0:T(8,128)(2,1)}, u32[]{:S(2)}, u32[]{:S(2)}) async-start(bf16[8,256,128]{2,1,0:T(8,128)(2,1)} %fusion.103), calls=%async_computation.1 | async-start | bytes 1048576 | tf_op jit(solution)/shard_map/all_to_all | solution.py:77
  93.1 49.1 %reduce-scatter.3.cloned.1.call-start = ((), (), s32[]{:S(2)}) async-start(), calls=%async_computation.7 | async-start | bytes 2621440 | tf_op jit(solution)/shard_map/reduce_scatter | solution.py:91
  93.2 4.5 copy-start.9
  109.9 2.7 copy-start.10
  112.6 1.6 copy-start.3
  112.6 147.9 %all-gather.7.cloned.1.call-start = ((), (), s32[]{:S(2)}) async-start(), calls=%async_computation.9 | async-start | bytes 10813440 | tf_op jit(solution)/shard_map/all_gather | solution.py:140
  149.6 118.3 %all-to-all-start.2 = ((bf16[32,48,768]{2,1,0:T(8,128)(2,1)}), bf16[32,48,768]{2,1,0:T(8,128)(2,1)}, u32[]{:S(2)}, u32[]{:S(2)}) async-start(bf16[32,48,768]{2,1,0:T(8,128)(2,1)} %convolution_convert_fusion.3), calls=%async_computation.3 | async-start | bytes 4718592 | tf_op jit(solution)/shard_map/all_to_all | solution.py:141
  154.4 327.9 %reduce-scatter.5.cloned.1.call-start = ((), (), s32[]{:S(2)}) async-start(), calls=%async_computation.8 | async-start | bytes 8650752 | tf_op jit(solution)/shard_map/reduce_scatter | solution.py:180
  272.4 7.1 %slice-start.2 = ((s8[8388608]{0:T(1024)(128)(4,1)}), s8[4194304]{0:T(1024)(128)(4,1)S(1)}, s32[]{:S(2)}) async-start(s8[8388608]{0:T(1024)(128)(4,1)} %bitcast.221), calls=%async_computation.12 | async-start | bytes 8388608
  275.9 3.5 slice-start.3
  279.5 3.6 slice-start.4
  281.3 2.3 slice-start.5
  281.3 6.2 %slice-start.6 = ((s8[8388608]{0:T(1024)(128)(4,1)}), s8[4194304]{0:T(1024)(128)(4,1)S(1)}, s32[]{:S(2)}) async-start(s8[8388608]{0:T(1024)(128)(4,1)} %bitcast.225), calls=%async_computation.16 | async-start | bytes 8388608
  283.6 3.9 slice-start.7
  285.5 17.0 %copy-start.4 = (bf16[768,512]{1,0:T(8,128)(2,1)}, bf16[768,512]{1,0:T(8,128)(2,1)S(1)}, u32[]{:S(2)}) copy-start(bf16[768,512]{1,0:T(8,128)(2,1)S(1)} %multiply_convert_fusion.3) | copy-start | bytes 2359300
  287.5 13.0 %slice-start = ((s8[8388608]{0:T(1024)(128)(4,1)}), s8[4194304]{0:T(1024)(128)(4,1)S(1)}, s32[]{:S(2)}) async-start(s8[8388608]{0:T(1024)(128)(4,1)} %bitcast.197), calls=%async_computation.10 | async-start | bytes 8388608
  289.5 14.1 %copy-start.6 = (bf16[768,512]{1,0:T(8,128)(2,1)}, bf16[768,512]{1,0:T(8,128)(2,1)S(1)}, u32[]{:S(2)}) copy-start(bf16[768,512]{1,0:T(8,128)(2,1)S(1)} %multiply_convert_fusion.1) | copy-start | bytes 2359300
  289.5 11.1 %slice-start.1 = ((s8[8388608]{0:T(1024)(128)(4,1)}), s8[4194304]{0:T(1024)(128)(4,1)S(1)}, s32[]{:S(2)}) async-start(s8[8388608]{0:T(1024)(128)(4,1)} %bitcast.197), calls=%async_computation.11 | async-start | bytes 8388608
  313.1 2.3 copy-start.5
  315.4 2.3 copy-start.7
  322.0 90.3 %all-to-all-start.3 = ((bf16[32,48,1024]{2,1,0:T(8,128)(2,1)}), bf16[32,48,1024]{2,1,0:T(8,128)(2,1)}, u32[]{:S(2)}, u32[]{:S(2)}) async-start(bf16[32,48,1024]{2,1,0:T(8,128)(2,1)} %bitcast.195), calls=%async_computation.5 | async-start | bytes 6291456 | tf_op jit(solution)/shard_map/all_to_all | solution.py:181
  412.3 75.6 %copy-start.1 = (bf16[512,2048]{1,0:T(8,128)(2,1)S(1)}, bf16[512,2048]{1,0:T(8,128)(2,1)}, u32[]{:S(2)}) copy-start(bf16[512,2048]{1,0:T(8,128)(2,1)} %param.19) | copy-start | bytes 6291460
Sparse Core Ops, SparseCore 0:
  8.9 26.2 all-gather.4
  112.7 29.5 reduce-scatter.2
  146.2 114.2 all-gather.6
  311.1 171.2 reduce-scatter.4
